TPU v7x, 768 devices: a whole 4x8x12 slice. The times are simulated.
768 devices in a mesh: expert: 8 (over y), dp: 96 (over x, z, core).
Axes of the slice: x: 4, y: 8, z: 12, core: 2. Of those that a mesh axis runs over, the one named last changes fastest.
Arguments:
- out_grad: bfloat16 [98304, 2048], P(('expert', 'dp')), may hold values from -6 to 6
- routes: int32 [98304, 6], P(('expert', 'dp')), may hold values from 0 to 63, all different within a row; in each aligned block of 128 rows (0 to 127, 128 to 255, ...) at most 32 rows name the same one
- gates: float32 [98304, 6], P(('expert', 'dp')), may hold values from 0.1 to 1
- saved_hidden: bfloat16 [8, 96, 8, 32, 768], P('expert', 'dp'), may hold values from -20 to 20
- down_weight: bfloat16 [8, 768, 2048], P('expert'), may hold values from -0.125 to 0.125
Outputs:
- d_hidden: bfloat16 [98304, 6, 768], P(('expert', 'dp'))
- weight_grad: float32 [8, 768, 2048], P('expert', 'dp')
Inputs may be any that keep to these rules, and one draw needn't show every extreme that they name: `routes`: each token names 6 different experts; among the tokens of one device no expert is named by more than 32 slots, a bound that some block reaches. Entries of saved_hidden at positions that no live slot takes are not read.
All inputs are finite; a program needn't handle non-finite values.
Results may differ from a plain program's by a relative error of at most 0.0049.
Values may be sent and summed in bfloat16 or wider, within the bound.
A program may use at most 64 MiB of HBM per device.

v0:
```python
import math

import jax
import jax.numpy as jnp
from jax import lax
from jax.sharding import PartitionSpec as P

EXPERTS_ALL = 64


def grad_rows(hidden_rows, columns):
    return lax.dot_general(
        hidden_rows, columns, (((0,), (0,)), ((), ())), preferred_element_type=jnp.float32
    )


def on_device(out_grad, routes, gates, saved_hidden, down_weight):
    experts_here = lax.axis_size("expert")
    tok_count = out_grad.shape[0]
    top_count = routes.shape[1]
    capacity = saved_hidden.shape[3]
    width = out_grad.shape[1]
    units = down_weight.shape[1]
    grad_scale = 1.0 / math.sqrt(
        tok_count * experts_here * lax.axis_size("dp") * top_count / EXPERTS_ALL
    )
    flat_routes = routes.reshape(-1)
    inside = flat_routes < experts_here
    onehot = (flat_routes[:, None] == jnp.arange(experts_here, dtype=jnp.int32)[None, :]).astype(
        jnp.int32
    )
    position = jnp.sum((jnp.cumsum(onehot, axis=0) - onehot) * onehot, axis=1)
    target = jnp.where(inside, flat_routes * capacity + position, experts_here * capacity)
    scaled = (gates[:, :, None] * out_grad[:, None, :].astype(jnp.float32)).astype(jnp.bfloat16)
    scaled = scaled.reshape(tok_count * top_count, width)
    outgoing = jnp.zeros((experts_here * capacity + 1, width), jnp.bfloat16).at[target].set(scaled)
    outgoing = outgoing[: experts_here * capacity].reshape(experts_here, capacity, width)
    weight = down_weight[0]
    hidden_rows = saved_hidden.reshape(-1, units)
    received = lax.all_to_all(outgoing, "expert", split_axis=0, concat_axis=0, tiled=True)
    recv_rows = received.reshape(-1, width)
    hidden_grad = jnp.einsum("scd,fd->scf", received, weight, preferred_element_type=jnp.float32)
    returned = lax.all_to_all(
        hidden_grad.astype(jnp.bfloat16), "expert", split_axis=0, concat_axis=0, tiled=True
    )
    summed = lax.psum_scatter(
        grad_rows(hidden_rows, recv_rows), "dp", scatter_dimension=0, tiled=True
    )
    flat_back = returned.reshape(-1, units)
    clamped = jnp.minimum(target, experts_here * capacity - 1)
    picked = flat_back[clamped]
    slot_grads = jnp.where(inside[:, None], picked, jnp.zeros_like(picked))
    d_hidden = slot_grads.reshape(tok_count, top_count, units)
    weight_grad = (summed * grad_scale)[None]
    return (d_hidden, weight_grad)


def solution(mesh):
    return jax.shard_map(
        on_device,
        mesh=mesh,
        in_specs=(
            P(("expert", "dp"), None),
            P(("expert", "dp"), None),
            P(("expert", "dp"), None),
            P("expert", "dp", None, None, None),
            P("expert", None, None),
        ),
        out_specs=(P(("expert", "dp"), None, None), P("expert", "dp", None)),
        check_vma=False,
    )
```

profile of v0, /device:TPU:32, one launch (start us, length us, event | category | flops | bytes accessed | tf_op | source)
XLA Modules:
  0.0 320.5 jit_solution(10544444661688854830)
XLA Ops:
  7.2 0.0 copy-start
  7.2 0.0 reduce-scatter.4.cloned.1.call-start
  7.2 0.9 copy.24
  8.2 0.1 eq.29
  8.3 0.1 eq.25
  8.4 0.7 broadcast_compare_fusion
  9.1 0.7 broadcast_multiply_fusion
  9.8 1.7 reduce-window.6
  11.5 0.1 slice.14
  11.6 0.1 copy.26
  11.7 0.2 reduce-window.9
  11.9 0.1 copy.27
  12.0 0.1 copy.21
  12.1 0.2 lt.45
  12.3 0.1 copy.23
  12.4 0.1 mul.49
  12.5 5.3 %mul.53 = f32[128,6,2048]{2,1,0:T(8,128)} broadcast(bf16[128,2048]{1,0:T(8,128)(2,1)} %param.5), dimensions={0,2} | broadcast | bytes 6815744 | tf_op jit(solution)/shard_map/mul | solution.py:34
  17.9 0.0 copy-start.3
  17.9 8.3 %mul.54 = f32[768,2048]{1,0:T(8,128)} reshape(f32[128,6,2048]{2,1,0:T(8,128)} %mul.53) | data formatting | bytes 12582912 | tf_op jit(solution)/shard_map/mul | solution.py:34
  26.1 0.0 copy-done.3
  26.1 0.1 copy.28
  26.3 0.1 mul.51
  26.4 0.1 fusion.9
  26.5 0.6 fusion.12
  27.1 12.8 %scatter_custom_fusion = bf16[257,2048]{1,0:T(8,128)(2,1)} fusion(s32[768]{0:T(1024)S(1)} %get-tuple-element.9, f32[768,2048]{1,0:T(8,128)} %mul.54, f32[768]{0:T(1024)S(1)} %mul.51, bf16[]{:T(256)} %constant.9.clone.1), kind=kCustom, calls=%fused_computation.4 | custom fusion | flops 3145728 | bytes 7348226 | tf_op jit(solution)/shard_map/scatter | solution.py:36
  39.9 0.0 copy-start.2
  39.9 1.3 slice.15
  41.2 30.4 %all_to_all.10 = bf16[8,32,2048]{2,1,0:T(8,128)(2,1)S(1)} all-to-all(bf16[8,32,2048]{2,1,0:T(8,128)(2,1)S(1)} %bitcast.30), channel_id=1, replica_groups=mesh['expert'=8,'dp'=96] {'expert'}, dimensions={0} | all-to-all | bytes 2097152 | tf_op jit(solution)/shard_map/all_to_all | solution.py:40
  71.6 0.0 copy-start.1
  71.6 1.0 copy-done.1
  72.6 0.0 copy-done.2
  72.6 3.7 %convolution_bitcast_fusion = f32[768,2048]{0,1:T(8,128)} fusion(bf16[256,2048]{1,0:T(8,128)(2,1)S(1)} %bitcast.29, bf16[256,768]{1,0:T(8,128)(2,1)S(1)} %bitcast.31), kind=kOutput, calls=%fused_computation.3 | convolution fusion | flops 805306368 | bytes 7733248 | tf_op jit(solution)/shard_map/dot_general | solution.py:12
  76.3 6.6 %copy.31 = f32[768,2048]{1,0:T(8,128)} copy(f32[768,2048]{0,1:T(8,128)} %convolution_bitcast_fusion) | data formatting | bytes 12582912
  82.9 0.0 reduce-scatter.4.cloned.1.call-update
  82.9 0.0 copy-done
  82.9 3.0 fusion.4
  85.9 8.7 %all-to-all-start.1 = ((bf16[8,32,768]{2,1,0:T(8,128)(2,1)}), bf16[8,32,768]{2,1,0:T(8,128)(2,1)S(1)}, u32[]{:S(2)}, u32[]{:S(2)}) async-start(bf16[8,32,768]{2,1,0:T(8,128)(2,1)} %fusion.4), calls=%async_computation.1 | async-start | bytes 786432 | tf_op jit(solution)/shard_map/all_to_all | solution.py:43
  94.7 1.3 pad_clamp_fusion
  96.0 5.2 %all-to-all-done.1 = bf16[8,32,768]{2,1,0:T(8,128)(2,1)S(1)} async-done(((bf16[8,32,768]{2,1,0:T(8,128)(2,1)}), bf16[8,32,768]{2,1,0:T(8,128)(2,1)S(1)}, u32[]{:S(2)}, u32[]{:S(2)}) %all-to-all-start.1) | async-done | bytes 393248 | tf_op jit(solution)/shard_map/all_to_all | solution.py:43
  101.2 3.6 %gather_fusion = bf16[768,768]{1,0:T(8,128)(2,1)} fusion(bf16[256,768]{1,0:T(8,128)(2,1)S(1)} %bitcast.28, s32[1024]{0:T(1024)} %pad_clamp_fusion), kind=kCustom, calls=%fused_computation | custom fusion | bytes 2362368 | tf_op jit(solution)/shard_map/gather | solution.py:51
  104.8 3.2 gather.6
  108.0 1.7 broadcast_select_fusion
  109.6 1.2 copy.29
  110.8 196.1 %reduce-scatter.4.cloned.1.call-done = f32[8,2048]{1,0:T(8,128)} async-done(((f32[768,2048]{1,0:T(8,128)}), f32[8,2048]{1,0:T(8,128)}) %reduce-scatter.4.cloned.1.call-update) | async-done | bytes 65552
  307.0 2.2 copy.32
  309.2 2.3 multiply_bitcast_fusion
  311.5 2.2 copy.30
  (1 shorter events, 0.0 us)
Async XLA Ops:
  7.2 75.7 %copy-start = (bf16[1,768,2048]{2,1,0:T(8,128)(2,1)S(1)}, bf16[1,768,2048]{2,1,0:T(8,128)(2,1)}, u32[]{:S(2)}) copy-start(bf16[1,768,2048]{2,1,0:T(8,128)(2,1)} %param.9) | copy-start | bytes 9437188
  7.2 299.8 %reduce-scatter.4.cloned.1.call-start = ((), (), s32[]{:S(2)}) async-start(), calls=%async_computation.3 | async-start | bytes 6356992
  17.9 8.3 %copy-start.3 = (f32[128,6]{0,1:T(8,128)S(1)}, f32[128,6]{0,1:T(8,128)}, u32[]{:S(2)}) copy-start(f32[128,6]{0,1:T(8,128)} %param.7) | copy-start | bytes 9220
  39.9 32.7 %copy-start.2 = (bf16[1,1,8,32,768]{4,3,2,1,0:T(8,128)(2,1)S(1)}, bf16[1,1,8,32,768]{4,3,2,1,0:T(8,128)(2,1)}, u32[]{:S(2)}) copy-start(bf16[1,1,8,32,768]{4,3,2,1,0:T(8,128)(2,1)} %param.8) | copy-start | bytes 1179652
  71.6 1.0 copy-start.1
  85.9 15.3 %all-to-all-start.1 = ((bf16[8,32,768]{2,1,0:T(8,128)(2,1)}), bf16[8,32,768]{2,1,0:T(8,128)(2,1)S(1)}, u32[]{:S(2)}, u32[]{:S(2)}) async-start(bf16[8,32,768]{2,1,0:T(8,128)(2,1)} %fusion.4), calls=%async_computation.1 | async-start | bytes 786432 | tf_op jit(solution)/shard_map/all_to_all | solution.py:43
Sparse Core Ops, SparseCore 0:
  83.0 223.9 reduce-scatter.3
where the time goes:
time: 322 us; the launch traced here: 320 us
  waiting for transfers between devices  201 us (62%)
  local copies, waits for them, and re-layouts  37.1 us (12%)
  blocking collectives  30.4 us (9%)
  other arithmetic  22 us (7%)
  between operations  14.1 us (4%)
  starting transfers between devices  8.78 us (3%)
  matrix products  6.71 us (2%)
    unnamed x2, waiting for transfers between devices  196 us
    all_to_all x1, blocking collectives, on_device(): lax.all_to_all(outgoing, 'expert', split_axis=0, concat_axis=0, tiled=True)  30.4 us
    unnamed x14, local copies, waits for them, and re-layouts  14.2 us
    mul x3, local copies, waits for them, and re-layouts, on_device(): gates[:, :, None] * out_grad[:, None, :].astype(jnp.float32)  13.7 us
    scatter x1, other arithmetic, on_device(): jnp.zeros((experts_here * capacity + 1, width), jnp.bfloat16).at[target]  12.8 us
    all_to_all x1, starting transfers between devices, on_device(): lax.all_to_all(hidden_grad.astype(jnp.bfloat16), 'expert', split_axis=0,...  8.74 us
    gather x2, local copies, waits for them, and re-layouts, on_device(): picked = flat_back[clamped]  6.77 us
  transfers between devices with their start and end apart: 2, of which 2 were waited for; matrix products, arithmetic and copies ran while one was open for 4% of the time, Pallas kernels for 0%

commit v1 on v0

v1 whole, which is shorter than its diff:
```python
import functools
import math

import jax
import jax.numpy as jnp
from jax import lax
from jax.experimental import pallas as pl
from jax.experimental.pallas import tpu as pltpu
from jax.sharding import PartitionSpec as P

EXPERTS_ALL = 64
MESH = pl.DeviceIdType.MESH
NY, NX, NZ, NC = 8, 4, 12, 2
CAP = 32
TOK = 128
TOP = 6
D = 2048
FF = 768
NCH = 8
CW = D // NCH
HW = CW // 2
Y_ORDER = (4, 3, 5, 2, 6, 1, 7)
X_ORDER = (2, 1, 3)
Z_ORDER = (6, 5, 7, 4, 8, 3, 9, 2, 10, 1, 11)
F32, BF16 = jnp.float32, jnp.bfloat16


def kernel(
    scale,
    og_hbm, rt_ref, gt_ref, hid_hbm, w_hbm,
    dh_hbm, wg_hbm,
    og, hid, hid_t, wv, outb, recv, acc, back, got, pick, dh,
    wg, cr, xf, xs, xr, zf, zs, zr, wgo,
    in_sem, w_sem, out_sem,
    ys_sem, yr_sem, bs_sem, br_sem, cs_sem, cr_sem, xs_sem, xr_sem, zs_sem, zr_sem,
):
    y = lax.axis_index("expert")
    dp = lax.axis_index("dp")
    c = lax.rem(dp, NC)
    z = lax.rem(dp // NC, NZ)
    x = dp // (NC * NZ)

    def dev_y(d):
        return (lax.rem(y + d, NY), dp)

    def dev_c():
        return (y, dp + 1 - 2 * c)

    def dev_x(d):
        return (y, (lax.rem(x + d, NX) * NZ + z) * NC + c)

    def dev_z(d):
        return (y, (x * NZ + lax.rem(z + d, NZ)) * NC + c)

    barrier = pltpu.get_barrier_semaphore()
    peers = [dev_z(d) for d in Z_ORDER] + [dev_y(d) for d in Y_ORDER]
    peers += [dev_x(d) for d in X_ORDER] + [dev_c()]
    for p in peers:
        pl.semaphore_signal(barrier, inc=1, device_id=p, device_id_type=MESH)

    def remote(src, dst, ssem, rsem, dev):
        return pltpu.make_async_remote_copy(
            src_ref=src, dst_ref=dst, send_sem=ssem, recv_sem=rsem,
            device_id=dev, device_id_type=MESH,
        )

    def disp(ch, d):
        return remote(
            outb.at[ch, lax.rem(y + d, NY)], recv.at[ch, y],
            ys_sem.at[ch, d - 1], yr_sem.at[ch, d - 1], dev_y(d),
        )

    def ret(d):
        return remote(
            back.at[lax.rem(y + d, NY)], got.at[y], bs_sem.at[d - 1], br_sem.at[d - 1], dev_y(d)
        )

    def core(ch):
        return remote(wg.at[ch, :, 1 - c], cr.at[ch], cs_sem.at[ch], cr_sem.at[ch], dev_c())

    def xcopy(ch, d):
        return remote(
            xs.at[ch, lax.rem(x + d, NX)], xr.at[ch, d - 1],
            xs_sem.at[ch, d - 1], xr_sem.at[ch, d - 1], dev_x(d),
        )

    def zcopy(ch, d):
        return remote(
            zs.at[ch, lax.rem(z + d, NZ)], zr.at[ch, d - 1],
            zs_sem.at[ch, d - 1], zr_sem.at[ch, d - 1], dev_z(d),
        )

    cp_og = pltpu.make_async_copy(og_hbm, og, in_sem.at[0])
    cp_og.start()
    cp_hid = pltpu.make_async_copy(hid_hbm, hid, in_sem.at[1])
    cp_hid.start()
    cp_w = []
    for ch in range(NCH):
        cp = pltpu.make_async_copy(w_hbm.at[:, pl.ds(ch * CW, CW)], wv.at[ch], w_sem.at[ch])
        cp.start()
        cp_w.append(cp)

    routes = rt_ref[...]
    gates = gt_ref[...]
    eid = lax.broadcasted_iota(jnp.int32, (NY, TOK), 0)
    mask = jnp.zeros((NY, TOK), F32)
    gate_e = jnp.zeros((NY, TOK), F32)
    for k in range(TOP):
        hit = routes[k : k + 1, :] == eid
        mask = mask + jnp.where(hit, 1.0, 0.0)
        gate_e = gate_e + jnp.where(hit, gates[k : k + 1, :], 0.0)
    t_row = lax.broadcasted_iota(jnp.int32, (TOK, TOK), 0)
    t_col = lax.broadcasted_iota(jnp.int32, (TOK, TOK), 1)
    before = jnp.where(t_row < t_col, 1.0, 0.0).astype(BF16)
    pos = jnp.dot(mask.astype(BF16), before, preferred_element_type=F32)
    slot = jnp.where(mask > 0.0, pos, -1.0).astype(jnp.int32)
    cid = lax.broadcasted_iota(jnp.int32, (NY, CAP, TOK), 1)
    sel = jnp.where(slot[:, None, :] == cid, 1.0, 0.0)
    gate_row = jnp.sum(sel * gate_e[:, None, :], axis=-1, keepdims=True).reshape(NY * CAP, 1)
    sel = sel.reshape(NY * CAP, TOK).astype(BF16)

    cp_og.wait()
    for ch in range(NCH):
        rows = jnp.dot(sel, og[:, ch * CW : (ch + 1) * CW], preferred_element_type=F32)
        outb[ch] = (rows * gate_row).astype(BF16).reshape(NY, CAP, CW)
        if ch == 0:
            pl.semaphore_wait(barrier, len(peers))
        for d in Y_ORDER:
            disp(ch, d).start()

    for ch in range(NCH):
        recv[ch, y] = outb[ch, y]
    rid = lax.broadcasted_iota(jnp.int32, (NY * CAP, TOK), 0)
    for k in range(TOP):
        hit = routes[k : k + 1, :] == eid
        pos_k = jnp.sum(jnp.where(hit, pos, 0.0), axis=0, keepdims=True).astype(jnp.int32)
        r_k = routes[k : k + 1, :]
        target = jnp.where(r_k < NY, r_k * CAP + pos_k, -1)
        pick[k] = jnp.where(rid == target, 1.0, 0.0).T.astype(BF16)
    cp_hid.wait()
    hid_t[...] = hid[...].T

    def stage_core(ch):
        core(ch).wait_recv()
        s = wg[ch, :, c] + cr[ch]
        s = jnp.concatenate([s[:, :, :HW], s[:, :, HW:]], axis=1)
        s = s.reshape(NX, NZ, 16, HW)
        xf[ch] = s
        xs[ch] = s.astype(BF16)
        for d in X_ORDER:
            xcopy(ch, d).start()

    def stage_x(ch):
        for d in X_ORDER:
            xcopy(ch, d).wait_recv()
        s = xf[ch, x]
        for d in X_ORDER:
            s = s + xr[ch, d - 1].astype(F32)
        zf[ch] = s
        zs[ch] = s.astype(BF16)
        for d in Z_ORDER:
            zcopy(ch, d).start()

    def stage_z(ch):
        for d in Z_ORDER:
            zcopy(ch, d).wait_recv()
        s = zf[ch, z]
        for d in Z_ORDER:
            s = s + zr[ch, d - 1].astype(F32)
        s = s * scale
        wgo[:, ch * CW : ch * CW + HW] = s[:8]
        wgo[:, ch * CW + HW : (ch + 1) * CW] = s[8:]

    for ch in range(NCH):
        for d in Y_ORDER:
            disp(ch, d).wait_recv()
        cp_w[ch].wait()
        rows = recv[ch].reshape(NY * CAP, CW)
        part = lax.dot_general(
            rows, wv[ch], (((1,), (1,)), ((), ())), preferred_element_type=F32
        )
        if ch == 0:
            acc[...] = part
        elif ch < NCH - 1:
            acc[...] += part
        else:
            back[...] = (acc[...] + part).astype(BF16).reshape(NY, CAP, FF)
            for d in Y_ORDER:
                ret(d).start()
        term = jnp.dot(hid_t[...], rows, preferred_element_type=F32)
        wg[ch] = term.reshape(NX * NZ, NC, 8, CW)
        core(ch).start()
        if ch >= 1:
            stage_core(ch - 1)
        if ch >= 2:
            stage_x(ch - 2)
        if ch >= 4:
            stage_z(ch - 4)
    got[y] = back[y]
    stage_core(NCH - 1)
    stage_x(NCH - 2)
    stage_x(NCH - 1)
    for ch in range(NCH - 4, NCH - 1):
        stage_z(ch)

    for d in Y_ORDER:
        ret(d).wait_recv()
    rows = got[...].reshape(NY * CAP, FF)
    outs = []
    for k in range(TOP):
        dh[k] = jnp.dot(pick[k], rows, preferred_element_type=F32).astype(BF16)
        cp = pltpu.make_async_copy(dh.at[k], dh_hbm.at[k], out_sem.at[k])
        cp.start()
        outs.append(cp)
    stage_z(NCH - 1)
    cp = pltpu.make_async_copy(wgo, wg_hbm, out_sem.at[TOP])
    cp.start()
    outs.append(cp)

    for ch in range(NCH):
        for d in Y_ORDER:
            disp(ch, d).wait_send()
        core(ch).wait_send()
        for d in X_ORDER:
            xcopy(ch, d).wait_send()
        for d in Z_ORDER:
            zcopy(ch, d).wait_send()
    for d in Y_ORDER:
        ret(d).wait_send()
    for cp in outs:
        cp.wait()


def on_device(out_grad, routes, gates, saved_hidden, down_weight):
    scale = 1.0 / math.sqrt(TOK * NY * NX * NZ * NC * TOP / EXPERTS_ALL)
    any_ = pl.BlockSpec(memory_space=pl.ANY)
    vmem = pl.BlockSpec(memory_space=pltpu.VMEM)
    dma = pltpu.SemaphoreType.DMA
    dh, wg = pl.pallas_call(
        functools.partial(kernel, scale),
        out_shape=(
            jax.ShapeDtypeStruct((TOP, TOK, FF), BF16),
            jax.ShapeDtypeStruct((8, D), F32),
        ),
        in_specs=[any_, vmem, vmem, any_, any_],
        out_specs=(any_, any_),
        scratch_shapes=[
            pltpu.VMEM((TOK, D), BF16),
            pltpu.VMEM((NY * CAP, FF), BF16),
            pltpu.VMEM((FF, NY * CAP), BF16),
            pltpu.VMEM((NCH, FF, CW), BF16),
            pltpu.VMEM((NCH, NY, CAP, CW), BF16),
            pltpu.VMEM((NCH, NY, CAP, CW), BF16),
            pltpu.VMEM((NY * CAP, FF), F32),
            pltpu.VMEM((NY, CAP, FF), BF16),
            pltpu.VMEM((NY, CAP, FF), BF16),
            pltpu.VMEM((TOP, TOK, NY * CAP), BF16),
            pltpu.VMEM((TOP, TOK, FF), BF16),
            pltpu.VMEM((NCH, NX * NZ, NC, 8, CW), F32),
            pltpu.VMEM((NCH, NX * NZ, 8, CW), F32),
            pltpu.VMEM((NCH, NX, NZ, 16, HW), F32),
            pltpu.VMEM((NCH, NX, NZ, 16, HW), BF16),
            pltpu.VMEM((NCH, NX - 1, NZ, 16, HW), BF16),
            pltpu.VMEM((NCH, NZ, 16, HW), F32),
            pltpu.VMEM((NCH, NZ, 16, HW), BF16),
            pltpu.VMEM((NCH, NZ - 1, 16, HW), BF16),
            pltpu.VMEM((8, D), F32),
            dma((2,)),
            dma((NCH,)),
            dma((TOP + 1,)),
            dma((NCH, NY - 1)),
            dma((NCH, NY - 1)),
            dma((NY - 1,)),
            dma((NY - 1,)),
            dma((NCH,)),
            dma((NCH,)),
            dma((NCH, NX - 1)),
            dma((NCH, NX - 1)),
            dma((NCH, NZ - 1)),
            dma((NCH, NZ - 1)),
        ],
        compiler_params=pltpu.CompilerParams(
            collective_id=0, has_side_effects=True, vmem_limit_bytes=48 << 20
        ),
        name="moe_down_bwd",
    )(
        out_grad,
        routes.T,
        gates.T,
        saved_hidden.reshape(NY * CAP, FF),
        down_weight[0],
    )
    return dh.transpose(1, 0, 2), wg[None]


def solution(mesh):
    return jax.shard_map(
        on_device,
        mesh=mesh,
        in_specs=(
            P(("expert", "dp"), None),
            P(("expert", "dp"), None),
            P(("expert", "dp"), None),
            P("expert", "dp", None, None, None),
            P("expert", None, None),
        ),
        out_specs=(P(("expert", "dp"), None, None), P("expert", "dp", None)),
        check_vma=False,
    )
```

time: 322 us -> 69.5 us (0.22)
  the two profiles are of different devices: /device:TPU:32 before, /device:TPU:1 now
where the time goes in v1:
time: 69.5 us; the launch traced here: 69.2 us
  Pallas kernels  61.6 us (89%)
  local copies, waits for them, and re-layouts  6.94 us (10%)
    pallas_call x1, Pallas kernels, on_device(): pl.pallas_call(functools.partial(kernel, scale), out_shape=(jax.ShapeDtyp...  61.6 us
    unnamed x12, local copies, waits for them, and re-layouts  6.94 us

profile of v1, /device:TPU:1, one launch (start us, length us, event | category | flops | bytes accessed | tf_op | source)
XLA Modules:
  0.0 69.2 jit_solution(5591458581424041455)
XLA Ops:
  0.6 0.0 copy-start
  0.6 1.9 %copy-done = bf16[1,768,2048]{2,1,0:T(8,128)(2,1)S(1)} copy-done((bf16[1,768,2048]{2,1,0:T(8,128)(2,1)S(1)}, bf16[1,768,2048]{2,1,0:T(8,128)(2,1)}, u32[]{:S(2)}) %copy-start) | copy-done | bytes 3145752
  2.5 0.0 copy-start.1
  2.5 1.0 %copy-done.1 = bf16[128,2048]{1,0:T(8,128)(2,1)S(1)} copy-done((bf16[128,2048]{1,0:T(8,128)(2,1)S(1)}, bf16[128,2048]{1,0:T(8,128)(2,1)}, u32[]{:S(2)}) %copy-start.1) | copy-done | bytes 524312
  3.6 0.0 copy-start.2
  3.6 1.0 %copy-done.2 = bf16[1,1,8,32,768]{4,3,2,1,0:T(8,128)(2,1)S(1)} copy-done((bf16[1,1,8,32,768]{4,3,2,1,0:T(8,128)(2,1)S(1)}, bf16[1,1,8,32,768]{4,3,2,1,0:T(8,128)(2,1)}, u32[]{:S(2)}) %copy-start.2) | copy-done | bytes 393240
  4.6 0.0 copy-start.3
  4.6 0.7 copy-done.3
  5.2 0.0 copy-start.4
  5.2 0.7 copy-done.4
  5.9 61.6 %moe_down_bwd.1 = (bf16[6,128,768]{2,1,0:T(8,128)(2,1)S(1)}, f32[8,2048]{1,0:T(8,128)S(1)}) custom-call(bf16[128,2048]{1,0:T(8,128)(2,1)S(1)} %copy-done.1, s32[6,128]{1,0:T(8,128)S(1)} %bitcast.10, f32[6,128]{1,0:T(8,128)S(1)} %bitcast.11, bf16[256,768]{1,0:T(8,128)(2,1)S(1)} %bitcast.8, bf16[768,2048]{1,0:T(8,128)(2,1)S(1)} %bitcast.6), custom_call_target="tpu_custom_call" | custom-call | tf_op jit(solution)/shard_map/moe_down_bwd/pallas_call | solution.py:239
  67.6 1.0 %copy.9 = bf16[128,6,768]{2,0,1:T(8,128)(2,1)} copy(bf16[128,6,768]{2,0,1:T(8,128)(2,1)S(1)} %bitcast.7) | data formatting | bytes 2359296
  68.6 0.6 copy.10
Async XLA Ops:
  0.6 1.9 %copy-start = (bf16[1,768,2048]{2,1,0:T(8,128)(2,1)S(1)}, bf16[1,768,2048]{2,1,0:T(8,128)(2,1)}, u32[]{:S(2)}) copy-start(bf16[1,768,2048]{2,1,0:T(8,128)(2,1)} %param.9) | copy-start | bytes 9437188
  2.5 1.0 %copy-start.1 = (bf16[128,2048]{1,0:T(8,128)(2,1)S(1)}, bf16[128,2048]{1,0:T(8,128)(2,1)}, u32[]{:S(2)}) copy-start(bf16[128,2048]{1,0:T(8,128)(2,1)} %og_hbm.1) | copy-start | bytes 1572868
  3.6 1.0 %copy-start.2 = (bf16[1,1,8,32,768]{4,3,2,1,0:T(8,128)(2,1)S(1)}, bf16[1,1,8,32,768]{4,3,2,1,0:T(8,128)(2,1)}, u32[]{:S(2)}) copy-start(bf16[1,1,8,32,768]{4,3,2,1,0:T(8,128)(2,1)} %param.8) | copy-start | bytes 1179652
  4.6 0.7 copy-start.3
  5.2 0.7 copy-start.4

commit v2 on v1

v2 whole, which is shorter than its diff:
```python
import functools
import math

import jax
import jax.numpy as jnp
from jax import lax
from jax.experimental import pallas as pl
from jax.experimental.pallas import tpu as pltpu
from jax.sharding import PartitionSpec as P

EXPERTS_ALL = 64
MESH = pl.DeviceIdType.MESH
NY, NX, NZ, NC = 8, 4, 12, 2
CAP = 32
TOK = 128
TOP = 6
D = 2048
FF = 768
WIDTHS = (256,) * 8
ZGROUPS = ((0, 1), (2, 3), (4, 5), (6,), (7,))
NCH = len(WIDTHS)
OFFS = tuple(sum(WIDTHS[:i]) for i in range(NCH))
NZG = len(ZGROUPS)
ZROWS = tuple(sum(WIDTHS[ch] // 16 for ch in g) for g in ZGROUPS)
VLIM = 62 << 20
Y_ORDER = (4, 3, 5, 2, 6, 1, 7)
X_ORDER = (2, 1, 3)
Z_ORDER = (6, 5, 7, 4, 8, 3, 9, 2, 10, 1, 11)
F32, BF16 = jnp.float32, jnp.bfloat16


def kernel(
    scale,
    og_hbm, rt_hbm, gt_hbm, hid_hbm, w_hbm,
    dh_hbm, wg_hbm,
    rt_ref, gt_ref, og, hid, hid_t, wv, outb, recv, acc, back, got, pick, dh,
    wg, cr, xf, xs, xr, zf, zs, zr, wgo,
    late_sem, in_sem, w_sem, out_sem,
    ys_sem, yr_sem, bs_sem, br_sem, cs_sem, cr_sem, xs_sem, xr_sem, zs_sem, zr_sem,
):
    y = lax.axis_index("expert")
    dp = lax.axis_index("dp")
    c = lax.rem(dp, NC)
    z = lax.rem(dp // NC, NZ)
    x = dp // (NC * NZ)

    def dev_y(d):
        return (lax.rem(y + d, NY), dp)

    def dev_c():
        return (y, dp + 1 - 2 * c)

    def dev_x(d):
        return (y, (lax.rem(x + d, NX) * NZ + z) * NC + c)

    def dev_z(d):
        return (y, (x * NZ + lax.rem(z + d, NZ)) * NC + c)

    def remote(src, dst, ssem, rsem, dev):
        return pltpu.make_async_remote_copy(
            src_ref=src, dst_ref=dst, send_sem=ssem, recv_sem=rsem,
            device_id=dev, device_id_type=MESH,
        )

    def disp(ch, d):
        return remote(
            outb[ch].at[lax.rem(y + d, NY)], recv[ch].at[y],
            ys_sem.at[ch, d - 1], yr_sem.at[ch, d - 1], dev_y(d),
        )

    def ret(d):
        return remote(
            back.at[lax.rem(y + d, NY)], got.at[y], bs_sem.at[d - 1], br_sem.at[d - 1], dev_y(d)
        )

    def core(ch):
        return remote(wg[ch].at[:, 1 - c], cr[ch], cs_sem.at[ch], cr_sem.at[ch], dev_c())

    def xcopy(ch, d):
        return remote(
            xs[ch].at[lax.rem(x + d, NX)], xr[ch].at[d - 1],
            xs_sem.at[ch, d - 1], xr_sem.at[ch, d - 1], dev_x(d),
        )

    def zcopy(g, d):
        return remote(
            zs[g].at[lax.rem(z + d, NZ)], zr[g].at[d - 1],
            zs_sem.at[g, d - 1], zr_sem.at[g, d - 1], dev_z(d),
        )

    cp_rt = pltpu.make_async_copy(rt_hbm, rt_ref, in_sem.at[2])
    cp_rt.start()
    cp_gt = pltpu.make_async_copy(gt_hbm, gt_ref, in_sem.at[3])
    cp_gt.start()
    cp_og = pltpu.make_async_copy(og_hbm, og, in_sem.at[0])
    cp_og.start()
    barrier = pltpu.get_barrier_semaphore()
    peers = [dev_y(d) for d in Y_ORDER] + [dev_x(d) for d in X_ORDER] + [dev_c()]
    for p in peers:
        pl.semaphore_signal(barrier, inc=1, device_id=p, device_id_type=MESH)
    for d in range(1, NZ):

        @pl.when(z + d < NZ)
        def _(d=d):
            pl.semaphore_signal(barrier, inc=1, device_id=dev_z(d), device_id_type=MESH)

    cp_hid = pltpu.make_async_copy(hid_hbm, hid, in_sem.at[1])
    cp_hid.start()
    cp_w = []
    for ch in range(NCH):
        cp = pltpu.make_async_copy(w_hbm.at[:, pl.ds(OFFS[ch], WIDTHS[ch])], wv[ch], w_sem.at[ch])
        cp.start()
        cp_w.append(cp)

    cp_rt.wait()
    cp_gt.wait()
    routes = rt_ref[...]
    gates = gt_ref[...]
    eid = lax.broadcasted_iota(jnp.int32, (NY, TOK), 0)
    mask = jnp.zeros((NY, TOK), F32)
    gate_e = jnp.zeros((NY, TOK), F32)
    for k in range(TOP):
        hit = routes[k : k + 1, :] == eid
        mask = mask + jnp.where(hit, 1.0, 0.0)
        gate_e = gate_e + jnp.where(hit, gates[k : k + 1, :], 0.0)
    t_row = lax.broadcasted_iota(jnp.int32, (TOK, TOK), 0)
    t_col = lax.broadcasted_iota(jnp.int32, (TOK, TOK), 1)
    before = jnp.where(t_row < t_col, 1.0, 0.0).astype(BF16)
    pos = jnp.dot(mask.astype(BF16), before, preferred_element_type=F32)
    slot = jnp.where(mask > 0.0, pos, -1.0).astype(jnp.int32)
    cid = lax.broadcasted_iota(jnp.int32, (NY, CAP, TOK), 1)
    sel = jnp.where(slot[:, None, :] == cid, 1.0, 0.0)
    gate_row = jnp.sum(sel * gate_e[:, None, :], axis=-1, keepdims=True).reshape(NY * CAP, 1)
    sel = sel.reshape(NY * CAP, TOK).astype(BF16)

    cp_og.wait()
    for ch in range(NCH):
        w = WIDTHS[ch]
        rows = jnp.dot(sel, og[:, OFFS[ch] : OFFS[ch] + w], preferred_element_type=F32)
        outb[ch][...] = (rows * gate_row).astype(BF16).reshape(NY, CAP, w)
        if ch == 0:
            pl.semaphore_wait(barrier, len(peers) + z)
        for d in Y_ORDER:
            disp(ch, d).start()

    for d in range(1, NZ):

        @pl.when(z >= d)
        def _(d=d):
            pl.semaphore_signal(late_sem, inc=1, device_id=dev_z(NZ - d), device_id_type=MESH)

    for ch in range(NCH):
        recv[ch][y] = outb[ch][y]
    rid = lax.broadcasted_iota(jnp.int32, (NY * CAP, TOK), 0)
    for k in range(TOP):
        hit = routes[k : k + 1, :] == eid
        pos_k = jnp.sum(jnp.where(hit, pos, 0.0), axis=0, keepdims=True).astype(jnp.int32)
        r_k = routes[k : k + 1, :]
        target = jnp.where(r_k < NY, r_k * CAP + pos_k, -1)
        pick[k] = jnp.where(rid == target, 1.0, 0.0).T.astype(BF16)
    cp_hid.wait()
    hid_t[...] = hid[...].T

    def stage_core(ch):
        w = WIDTHS[ch]
        core(ch).wait_recv()
        s = wg[ch][:, c] + cr[ch][...]
        s = jnp.concatenate([s[:, :, i : i + 128] for i in range(0, w, 128)], axis=1)
        xf[ch][...] = s.reshape(NX, NZ, w // 16, 128)
        xs[ch][...] = s.reshape(NX, NZ * w // 16, 128).astype(BF16)
        for d in X_ORDER:
            xcopy(ch, d).start()

    def stage_x(ch):
        w = WIDTHS[ch]
        for d in X_ORDER:
            xcopy(ch, d).wait_recv()
        s = xf[ch][x].reshape(NZ * w // 16, 128)
        for d in X_ORDER:
            s = s + xr[ch][d - 1].astype(F32)
        s = s.reshape(NZ, w // 16, 128)
        g = next(i for i in range(NZG) if ch in ZGROUPS[i])
        o = sum(WIDTHS[i] // 16 for i in ZGROUPS[g] if i < ch)
        zf[g][:, o : o + w // 16] = s
        if ch == ZGROUPS[g][-1]:
            zs[g][...] = zf[g][...].astype(BF16)
            if g == 0:

                @pl.when(z < NZ - 1)
                def _():
                    pl.semaphore_wait(late_sem, NZ - 1 - z)

            for d in Z_ORDER:
                zcopy(g, d).start()

    def stage_z(g):
        for d in Z_ORDER:
            zcopy(g, d).wait_recv()
        s = zf[g][z]
        for d in Z_ORDER:
            s = s + zr[g][d - 1].astype(F32)
        s = s * scale
        r = 0
        for ch in ZGROUPS[g]:
            for o in range(OFFS[ch], OFFS[ch] + WIDTHS[ch], 128):
                wgo[:, o : o + 128] = s[r : r + 8]
                r += 8

    def stage_d(ch):
        for d in Y_ORDER:
            disp(ch, d).wait_recv()
        rows = recv[ch][...].reshape(NY * CAP, WIDTHS[ch])
        term = jnp.dot(hid_t[...], rows, preferred_element_type=F32)
        wg[ch][...] = term.reshape(NX * NZ, NC, 8, WIDTHS[ch])
        core(ch).start()

    def stage_h(ch):
        cp_w[ch].wait()
        part = lax.dot_general(
            recv[ch][...].reshape(NY * CAP, WIDTHS[ch]), wv[ch][...],
            (((1,), (1,)), ((), ())), preferred_element_type=F32,
        )
        if ch == 0:
            acc[...] = part
        elif ch < NCH - 1:
            acc[...] += part
        else:
            back[...] = (acc[...] + part).astype(BF16).reshape(NY, CAP, FF)
            for d in Y_ORDER:
                ret(d).start()

    for ch in range(NCH):
        stage_d(ch)
        stage_h(ch)
        if ch >= 2:
            stage_x(ch - 2)
        stage_core(ch)
    stage_x(NCH - 2)
    stage_x(NCH - 1)
    got[y] = back[y]

    for d in Y_ORDER:
        ret(d).wait_recv()
    rows = got[...].reshape(NY * CAP, FF)
    outs = []
    for k in range(TOP):
        dh[k] = jnp.dot(pick[k], rows, preferred_element_type=F32).astype(BF16)
        cp = pltpu.make_async_copy(dh.at[k], dh_hbm.at[k], out_sem.at[k])
        cp.start()
        outs.append(cp)
    for ch in range(NCH):
        for d in Y_ORDER:
            disp(ch, d).wait_send()
        core(ch).wait_send()
        for d in X_ORDER:
            xcopy(ch, d).wait_send()
    for d in Y_ORDER:
        ret(d).wait_send()
    for g in range(NZG):
        for d in Z_ORDER:
            zcopy(g, d).wait_send()
    for g in range(NZG):
        stage_z(g)
    cp = pltpu.make_async_copy(wgo, wg_hbm, out_sem.at[TOP])
    cp.start()
    outs.append(cp)
    for cp in outs:
        cp.wait()


def on_device(out_grad, routes, gates, saved_hidden, down_weight):
    scale = 1.0 / math.sqrt(TOK * NY * NX * NZ * NC * TOP / EXPERTS_ALL)
    any_ = pl.BlockSpec(memory_space=pl.ANY)
    hbm = pl.BlockSpec(memory_space=pltpu.HBM)
    dma = pltpu.SemaphoreType.DMA
    dh, wg = pl.pallas_call(
        functools.partial(kernel, scale),
        out_shape=(
            jax.ShapeDtypeStruct((TOP, TOK, FF), BF16),
            jax.ShapeDtypeStruct((8, D), F32),
        ),
        in_specs=[hbm] * 5,
        out_specs=(any_, any_),
        scratch_shapes=[
            pltpu.VMEM((TOP, TOK), jnp.int32),
            pltpu.VMEM((TOP, TOK), F32),
            pltpu.VMEM((TOK, D), BF16),
            pltpu.VMEM((NY * CAP, FF), BF16),
            pltpu.VMEM((FF, NY * CAP), BF16),
            [pltpu.VMEM((FF, w), BF16) for w in WIDTHS],
            [pltpu.VMEM((NY, CAP, w), BF16) for w in WIDTHS],
            [pltpu.VMEM((NY, CAP, w), BF16) for w in WIDTHS],
            pltpu.VMEM((NY * CAP, FF), F32),
            pltpu.VMEM((NY, CAP, FF), BF16),
            pltpu.VMEM((NY, CAP, FF), BF16),
            pltpu.VMEM((TOP, TOK, NY * CAP), BF16),
            pltpu.VMEM((TOP, TOK, FF), BF16),
            [pltpu.VMEM((NX * NZ, NC, 8, w), F32) for w in WIDTHS],
            [pltpu.VMEM((NX * NZ, 8, w), F32) for w in WIDTHS],
            [pltpu.VMEM((NX, NZ, w // 16, 128), F32) for w in WIDTHS],
            [pltpu.VMEM((NX, NZ * w // 16, 128), BF16) for w in WIDTHS],
            [pltpu.VMEM((NX - 1, NZ * w // 16, 128), BF16) for w in WIDTHS],
            [pltpu.VMEM((NZ, r, 128), F32) for r in ZROWS],
            [pltpu.VMEM((NZ, r, 128), BF16) for r in ZROWS],
            [pltpu.VMEM((NZ - 1, r, 128), BF16) for r in ZROWS],
            pltpu.VMEM((8, D), F32),
            pltpu.SemaphoreType.REGULAR,
            dma((4,)),
            dma((NCH,)),
            dma((TOP + 1,)),
            dma((NCH, NY - 1)),
            dma((NCH, NY - 1)),
            dma((NY - 1,)),
            dma((NY - 1,)),
            dma((NCH,)),
            dma((NCH,)),
            dma((NCH, NX - 1)),
            dma((NCH, NX - 1)),
            dma((NZG, NZ - 1)),
            dma((NZG, NZ - 1)),
        ],
        compiler_params=pltpu.CompilerParams(
            collective_id=0, has_side_effects=True, vmem_limit_bytes=VLIM
        ),
        name="moe_down_bwd",
    )(
        out_grad,
        routes.T,
        gates.T,
        saved_hidden.reshape(NY * CAP, FF),
        down_weight[0],
    )
    return dh.transpose(1, 0, 2), wg[None]


def solution(mesh):
    return jax.shard_map(
        on_device,
        mesh=mesh,
        in_specs=(
            P(("expert", "dp"), None),
            P(("expert", "dp"), None),
            P(("expert", "dp"), None),
            P("expert", "dp", None, None, None),
            P("expert", None, None),
        ),
        out_specs=(P(("expert", "dp"), None, None), P("expert", "dp", None)),
        check_vma=False,
    )
```

time: 69.5 us -> 61.1 us (0.88)
  Pallas kernels: 61.6 us -> 57.2 us
  local copies, waits for them, and re-layouts: 6.94 us -> 3.02 us
    pallas_call x1, Pallas kernels: 61.6 us -> 57.2 us  [on_device(): pl.pallas_call(functools.partial(kernel, scale), out_shape=(jax.ShapeDtyp...]
    unnamed x12 -> x4, local copies, waits for them, and re-layouts: 6.94 us -> 3.02 us
where the time goes in v2:
time: 61.1 us; the launch traced here: 60.9 us
  Pallas kernels  57.2 us (94%)
  local copies, waits for them, and re-layouts  3.02 us (5%)
  between operations  0.65 us (1%)
    pallas_call x1, Pallas kernels, on_device(): pl.pallas_call(functools.partial(kernel, scale), out_shape=(jax.ShapeDtyp...  57.2 us
    unnamed x4, local copies, waits for them, and re-layouts  3.02 us

profile of v2, /device:TPU:1, one launch (start us, length us, event | category | flops | bytes accessed | tf_op | source)
XLA Modules:
  0.0 60.9 jit_solution(11071911607222339406)
XLA Ops:
  0.6 57.2 %moe_down_bwd.1 = (bf16[6,128,768]{2,1,0:T(8,128)(2,1)}, f32[8,2048]{1,0:T(8,128)}) custom-call(bf16[128,2048]{1,0:T(8,128)(2,1)} %og_hbm.1, s32[6,128]{1,0:T(8,128)} %bitcast.10, f32[6,128]{1,0:T(8,128)} %bitcast.11, bf16[256,768]{1,0:T(8,128)(2,1)} %bitcast.8, bf16[768,2048]{1,0:T(8,128)(2,1)} %bitcast.6), custom_call_target="tpu_custom_call" | custom-call | tf_op jit(solution)/shard_map/moe_down_bwd/pallas_call | solution.py:276
  57.9 0.0 copy-start
  57.9 2.4 %copy.9 = bf16[128,6,768]{2,0,1:T(8,128)(2,1)} copy(bf16[128,6,768]{2,0,1:T(8,128)(2,1)} %bitcast.7) | data formatting | bytes 2359296
  60.3 0.0 copy-done
  60.3 0.6 %copy.10 = f32[1,8,2048]{2,1,0:T(8,128)} copy(f32[1,8,2048]{2,1,0:T(8,128)S(1)} %bitcast.9) | data formatting | bytes 131072
Async XLA Ops:
  57.9 2.4 %copy-start = (f32[8,2048]{1,0:T(8,128)S(1)}, f32[8,2048]{1,0:T(8,128)}, u32[]{:S(2)}) copy-start(f32[8,2048]{1,0:T(8,128)} %get-tuple-element.5) | copy-start | bytes 196612

commit v3 on v2

--- a/solution.py
+++ b/solution.py
@@ -22,6 +22,7 @@
 OFFS = tuple(sum(WIDTHS[:i]) for i in range(NCH))
 NZG = len(ZGROUPS)
 ZROWS = tuple(sum(WIDTHS[ch] // 16 for ch in g) for g in ZGROUPS)
+UGRID = 2
 VLIM = 62 << 20
 Y_ORDER = (4, 3, 5, 2, 6, 1, 7)
 X_ORDER = (2, 1, 3)
@@ -32,8 +33,8 @@
 def kernel(
     scale,
     og_hbm, rt_hbm, gt_hbm, hid_hbm, w_hbm,
-    dh_hbm, wg_hbm,
-    rt_ref, gt_ref, og, hid, hid_t, wv, outb, recv, acc, back, got, pick, dh,
+    got_hbm, pick_hbm, wg_hbm,
+    rt_ref, gt_ref, og, hid, hid_t, wv, outb, recv, acc, back, got, pick,
     wg, cr, xf, xs, xr, zf, zs, zr, wgo,
     late_sem, in_sem, w_sem, out_sem,
     ys_sem, yr_sem, bs_sem, br_sem, cs_sem, cr_sem, xs_sem, xr_sem, zs_sem, zr_sem,
@@ -140,14 +141,14 @@
         outb[ch][...] = (rows * gate_row).astype(BF16).reshape(NY, CAP, w)
         if ch == 0:
             pl.semaphore_wait(barrier, len(peers) + z)
+            for d in range(1, NZ):
+
+                @pl.when(z >= d)
+                def _(d=d):
+                    pl.semaphore_signal(late_sem, inc=1, device_id=dev_z(NZ - d), device_id_type=MESH)
+
         for d in Y_ORDER:
             disp(ch, d).start()
-
-    for d in range(1, NZ):
-
-        @pl.when(z >= d)
-        def _(d=d):
-            pl.semaphore_signal(late_sem, inc=1, device_id=dev_z(NZ - d), device_id_type=MESH)
 
     for ch in range(NCH):
         recv[ch][y] = outb[ch][y]
@@ -159,6 +160,8 @@
         target = jnp.where(r_k < NY, r_k * CAP + pos_k, -1)
         pick[k] = jnp.where(rid == target, 1.0, 0.0).T.astype(BF16)
     cp_hid.wait()
+    cp_pick = pltpu.make_async_copy(pick, pick_hbm, out_sem.at[0])
+    cp_pick.start()
     hid_t[...] = hid[...].T
 
     def stage_core(ch):
@@ -241,13 +244,8 @@
 
     for d in Y_ORDER:
         ret(d).wait_recv()
-    rows = got[...].reshape(NY * CAP, FF)
-    outs = []
-    for k in range(TOP):
-        dh[k] = jnp.dot(pick[k], rows, preferred_element_type=F32).astype(BF16)
-        cp = pltpu.make_async_copy(dh.at[k], dh_hbm.at[k], out_sem.at[k])
-        cp.start()
-        outs.append(cp)
+    cp_got = pltpu.make_async_copy(got, got_hbm, out_sem.at[1])
+    cp_got.start()
     for ch in range(NCH):
         for d in Y_ORDER:
             disp(ch, d).wait_send()
@@ -261,11 +259,18 @@
             zcopy(g, d).wait_send()
     for g in range(NZG):
         stage_z(g)
-    cp = pltpu.make_async_copy(wgo, wg_hbm, out_sem.at[TOP])
-    cp.start()
-    outs.append(cp)
-    for cp in outs:
-        cp.wait()
+    cp_wg = pltpu.make_async_copy(wgo, wg_hbm, out_sem.at[2])
+    cp_wg.start()
+    cp_pick.wait()
+    cp_got.wait()
+    cp_wg.wait()
+
+
+def unpack(got_ref, pick_ref, sum_ref, dh_ref, wg_ref):
+    rows = got_ref[...]
+    for k in range(pick_ref.shape[0]):
+        dh_ref[k] = jnp.dot(pick_ref[k], rows, preferred_element_type=F32).astype(BF16)
+    wg_ref[...] = sum_ref[...]
 
 
 def on_device(out_grad, routes, gates, saved_hidden, down_weight):
@@ -273,14 +278,15 @@
     any_ = pl.BlockSpec(memory_space=pl.ANY)
     hbm = pl.BlockSpec(memory_space=pltpu.HBM)
     dma = pltpu.SemaphoreType.DMA
-    dh, wg = pl.pallas_call(
+    got, pick, wg = pl.pallas_call(
         functools.partial(kernel, scale),
         out_shape=(
-            jax.ShapeDtypeStruct((TOP, TOK, FF), BF16),
+            jax.ShapeDtypeStruct((NY, CAP, FF), BF16),
+            jax.ShapeDtypeStruct((TOP, TOK, NY * CAP), BF16),
             jax.ShapeDtypeStruct((8, D), F32),
         ),
         in_specs=[hbm] * 5,
-        out_specs=(any_, any_),
+        out_specs=(any_, any_, any_),
         scratch_shapes=[
             pltpu.VMEM((TOP, TOK), jnp.int32),
             pltpu.VMEM((TOP, TOK), F32),
@@ -294,7 +300,6 @@
             pltpu.VMEM((NY, CAP, FF), BF16),
             pltpu.VMEM((NY, CAP, FF), BF16),
             pltpu.VMEM((TOP, TOK, NY * CAP), BF16),
-            pltpu.VMEM((TOP, TOK, FF), BF16),
             [pltpu.VMEM((NX * NZ, NC, 8, w), F32) for w in WIDTHS],
             [pltpu.VMEM((NX * NZ, 8, w), F32) for w in WIDTHS],
             [pltpu.VMEM((NX, NZ, w // 16, 128), F32) for w in WIDTHS],
@@ -307,7 +312,7 @@
             pltpu.SemaphoreType.REGULAR,
             dma((4,)),
             dma((NCH,)),
-            dma((TOP + 1,)),
+            dma((3,)),
             dma((NCH, NY - 1)),
             dma((NCH, NY - 1)),
             dma((NY - 1,)),
@@ -330,6 +335,26 @@
         saved_hidden.reshape(NY * CAP, FF),
         down_weight[0],
     )
+    kb = TOP // UGRID
+    dh, wg = pl.pallas_call(
+        unpack,
+        grid=(UGRID,),
+        out_shape=(
+            jax.ShapeDtypeStruct((TOP, TOK, FF), BF16),
+            jax.ShapeDtypeStruct((8, D), F32),
+        ),
+        in_specs=[
+            pl.BlockSpec((NY * CAP, FF), lambda k: (0, 0)),
+            pl.BlockSpec((kb, TOK, NY * CAP), lambda k: (k, 0, 0)),
+            pl.BlockSpec((8, D), lambda k: (0, 0)),
+        ],
+        out_specs=(
+            pl.BlockSpec((kb, TOK, FF), lambda k: (k, 0, 0)),
+            pl.BlockSpec((8, D), lambda k: (0, 0)),
+        ),
+        compiler_params=pltpu.CompilerParams(vmem_limit_bytes=VLIM),
+        name="unpack",
+    )(got.reshape(NY * CAP, FF), pick, wg)
     return dh.transpose(1, 0, 2), wg[None]
 
 

time: 61.1 us -> 60.5 us (level)
  local copies, waits for them, and re-layouts: 3.02 us -> 0 us
  Pallas kernels: 57.2 us -> 59.7 us
    unnamed x4 -> x0, local copies, waits for them, and re-layouts: 3.02 us -> none
    pallas_call x0 -> x1, Pallas kernels: none -> 2.62 us  [on_device(): pl.pallas_call(unpack, grid=(UGRID,), out_shape=(jax.ShapeDtypeStruct((TO...]
where the time goes in v3:
time: 60.5 us; the launch traced here: 60.4 us
  Pallas kernels  59.7 us (99%)
  between operations  0.64 us (1%)
    pallas_call x1, Pallas kernels, on_device(): pl.pallas_call(functools.partial(kernel, scale), out_shape=(jax.ShapeDtyp...  57.1 us
    pallas_call x1, Pallas kernels, on_device(): pl.pallas_call(unpack, grid=(UGRID,), out_shape=(jax.ShapeDtypeStruct((TO...  2.62 us

profile of v3, /device:TPU:1, one launch (start us, length us, event | category | flops | bytes accessed | tf_op | source)
XLA Modules:
  0.0 60.4 jit_solution(17093683253462647726)
XLA Ops:
  0.6 57.1 %moe_down_bwd.1 = (bf16[8,32,768]{2,1,0:T(8,128)(2,1)}, bf16[6,128,256]{2,1,0:T(8,128)(2,1)}, f32[8,2048]{1,0:T(8,128)}) custom-call(bf16[128,2048]{1,0:T(8,128)(2,1)} %og_hbm.1, s32[6,128]{1,0:T(8,128)} %bitcast.10, f32[6,128]{1,0:T(8,128)} %bitcast.11, bf16[256,768]{1,0:T(8,128)(2,1)} %bitcast.9, bf16[768,2048]{1,0:T(8,128)(2,1)} %bitcast.7), custom_call_target="tpu_custom_call" | custom-call | tf_op jit(solution)/shard_map/moe_down_bwd/pallas_call | solution.py:281
  57.7 2.6 %unpack.1 = (bf16[6,128,768]{2,1,0:T(8,128)(2,1)}, f32[8,2048]{1,0:T(8,128)}) custom-call(bf16[256,768]{1,0:T(8,128)(2,1)} %bitcast.8, bf16[6,128,256]{2,1,0:T(8,128)(2,1)} %get-tuple-element.8.pick_ref, f32[8,2048]{1,0:T(8,128)} %get-tuple-element.9.sum_ref), custom_call_target="tpu_custom_call" | custom-call | tf_op jit(solution)/shard_map/unpack/pallas_call | solution.py:339

commit v4 on v3

--- a/solution.py
+++ b/solution.py
@@ -22,7 +22,7 @@
 OFFS = tuple(sum(WIDTHS[:i]) for i in range(NCH))
 NZG = len(ZGROUPS)
 ZROWS = tuple(sum(WIDTHS[ch] // 16 for ch in g) for g in ZGROUPS)
-UGRID = 2
+UGRID = 1
 VLIM = 62 << 20
 Y_ORDER = (4, 3, 5, 2, 6, 1, 7)
 X_ORDER = (2, 1, 3)

time: 60.5 us -> 60.5 us (level)
  no operation moved by 1% of the time
where the time goes in v4:
time: 60.5 us; the launch traced here: 60.4 us
  Pallas kernels  59.7 us (99%)
  between operations  0.64 us (1%)
    pallas_call x1, Pallas kernels, on_device(): pl.pallas_call(functools.partial(kernel, scale), out_shape=(jax.ShapeDtyp...  57.1 us
    pallas_call x1, Pallas kernels, on_device(): pl.pallas_call(unpack, grid=(UGRID,), out_shape=(jax.ShapeDtypeStruct((TO...  2.61 us

profile of v4, /device:TPU:1, one launch (start us, length us, event | category | flops | bytes accessed | tf_op | source)
XLA Modules:
  0.0 60.4 jit_solution(18327819247616338441)
XLA Ops:
  0.6 57.1 %moe_down_bwd.1 = (bf16[8,32,768]{2,1,0:T(8,128)(2,1)}, bf16[6,128,256]{2,1,0:T(8,128)(2,1)}, f32[8,2048]{1,0:T(8,128)}) custom-call(bf16[128,2048]{1,0:T(8,128)(2,1)} %og_hbm.1, s32[6,128]{1,0:T(8,128)} %bitcast.10, f32[6,128]{1,0:T(8,128)} %bitcast.11, bf16[256,768]{1,0:T(8,128)(2,1)} %bitcast.9, bf16[768,2048]{1,0:T(8,128)(2,1)} %bitcast.7), custom_call_target="tpu_custom_call" | custom-call | tf_op jit(solution)/shard_map/moe_down_bwd/pallas_call | solution.py:281
  57.7 2.6 %unpack.1 = (bf16[6,128,768]{2,1,0:T(8,128)(2,1)}, f32[8,2048]{1,0:T(8,128)}) custom-call(bf16[256,768]{1,0:T(8,128)(2,1)} %bitcast.8, bf16[6,128,256]{2,1,0:T(8,128)(2,1)} %get-tuple-element.8.pick_ref, f32[8,2048]{1,0:T(8,128)} %get-tuple-element.9.sum_ref), custom_call_target="tpu_custom_call" | custom-call | tf_op jit(solution)/shard_map/unpack/pallas_call | solution.py:339
